TPU v7x, 32 devices: a whole 2x2x4 slice. The times are simulated.
32 devices in a mesh: dp: 8 (over y, x, core), ctx: 4 (over z).
Axes of the slice: x: 2, y: 2, z: 4, core: 2. Of those that a mesh axis runs over, the one named last changes fastest.
Arguments:
- hidden: bfloat16 [8, 512, 4096], P('dp', 'ctx'), may hold values from -6 to 6
- dt_weight: bfloat16 [4096, 32], P('dp'), may hold values from -0.09375 to 0.09375
- ssm_input: bfloat16 [8, 512, 2048], P('dp', 'ctx'), may hold values from -6 to 6
- grad_output: bfloat16 [8, 512, 2048], P('dp', 'ctx'), may hold values from -1 to 1
- b_matrix: bfloat16 [8, 512, 1024], P('dp', 'ctx'), may hold values from -0.59765625 to 0.59765625
- c_matrix: bfloat16 [8, 512, 1024], P('dp', 'ctx'), may hold values from -0.59765625 to 0.59765625
- stored_states: bfloat16 [8, 4, 32, 64, 128], P('dp', 'ctx'), may hold values from -6 to 6
- step_bias: float32 [32], replicated, may hold values from -4 to 0.5
- decay_code: int32 [32], replicated, may hold values from 16 to 15872
- head_group: int32 [32], replicated, may hold values from 0 to 7
Outputs:
- grad_b: bfloat16 [8, 512, 1024], P('dp', 'ctx')
- grad_w: float32 [4096, 32], P('dp')
All inputs are finite; a program needn't handle non-finite values.
Results may differ from a plain program's by a relative error of at most 0.001.
Values may be sent and summed in bfloat16 or wider, within the bound.
A program may use at most 128 MiB of HBM per device.

v0:
```python
import functools

import jax
import jax.numpy as jnp
from jax import lax
from jax.experimental import pallas as pl
from jax.experimental.pallas import tpu as pltpu
from jax.sharding import PartitionSpec as P

HEADDIM = 64
NSTATE = 128
GROUPS = 8
CHUNK_HEADS = 4
FUSE_END = True

f32, bf16 = jnp.float32, jnp.bfloat16
MESH = pl.DeviceIdType.MESH
exact = lax.Precision.HIGHEST


def mm(a, b):
    return jnp.dot(a, b, preferred_element_type=f32)


def mm_nt(a, b):
    return lax.dot_general(a, b, (((1,), (1,)), ((), ())), preferred_element_type=f32)


def split(v):
    hi = v.astype(bf16)
    return hi, (v - hi.astype(f32)).astype(bf16)


def kernel(cfg, hid, w, x, cot, b, c, st, bias, code, hg, *rest):
    n_dp, n_ctx, gather, fuse = cfg
    (out_b, out_w), rest = rest[:2], rest[2:]
    (wall, cot_t, bg, cg2, sc, cum_s, last_s, growth_s, elast_s, cumb, stepb, acc,
     row_s, col_s, car_s, end_s, gs_s, send_s, recv_s, w_own,
     w_send, w_recv, ch_send, ch_recv) = rest[:24]
    length = x.shape[0]
    heads = bias.shape[1]
    depth = hid.shape[1] // n_dp
    full_length = length * n_ctx
    dp = lax.axis_index("dp")
    ctx = lax.axis_index("ctx")
    is_last = ctx == n_ctx - 1

    if fuse:
        hall, graw_own, graw_all, part, h_send, h_recv, g_send, g_recv, p_all, p_send, p_recv = rest[24:]

    barrier = pltpu.get_barrier_semaphore()
    if gather or fuse:
        for r in range(1, n_dp):
            pl.semaphore_signal(barrier, inc=1, device_id=(lax.rem(dp + r, n_dp), ctx), device_id_type=MESH)
    for r in range(1, n_ctx):
        pl.semaphore_signal(barrier, inc=1, device_id=(dp, lax.rem(ctx + r, n_ctx)), device_id_type=MESH)

    ri = lax.broadcasted_iota(jnp.int32, (heads, heads), 0)
    ci = lax.broadcasted_iota(jnp.int32, (heads, heads), 1)
    eye = ri == ci
    if gather:
        w_own[...] = mm_nt(eye.astype(bf16), w[...]).astype(bf16)
    pl.semaphore_wait(barrier, (n_dp - 1 if gather or fuse else 0) + n_ctx - 1)

    def w_copy(r, peer, slot):
        return pltpu.make_async_remote_copy(
            src_ref=w_own, dst_ref=wall.at[slot], send_sem=w_send.at[r], recv_sem=w_recv.at[r],
            device_id=(peer, ctx), device_id_type=MESH)

    def h_copy(r, peer, slot):
        return pltpu.make_async_remote_copy(
            src_ref=hid.at[:, pl.ds(pl.multiple_of(peer * depth, depth), depth)], dst_ref=hall.at[slot],
            send_sem=h_send.at[r], recv_sem=h_recv.at[r], device_id=(peer, ctx), device_id_type=MESH)

    if gather:
        for r in range(1, n_dp):
            w_copy(r, lax.rem(dp + r, n_dp), dp).start()
        wall[dp] = w_own[...]
    if fuse:
        for r in range(1, n_dp):
            h_copy(r, lax.rem(dp + r, n_dp), dp).start()
        hall[dp] = hid[:, pl.ds(pl.multiple_of(dp * depth, depth), depth)]

    for k in range(x.shape[1] // 128):
        cot_t[pl.ds(128 * k, 128), :] = cot[:, pl.ds(128 * k, 128)].T
    for g in range(GROUPS):
        b_g = b[:, pl.ds(NSTATE * g, NSTATE)]
        c_g = c[:, pl.ds(NSTATE * g, NSTATE)]
        bg[g] = b_g.astype(f32)
        cg2[g, :length, :] = c_g
        cg2[g, length:, :] = c_g
        sc[g] = mm_nt(b_g, c_g)
    acc[...] = jnp.zeros_like(acc)

    @pl.when(is_last)
    def _():
        recv_s[...] = jnp.zeros_like(recv_s)

    bias_c = jnp.sum(jnp.where(eye, bias[...], 0.0), axis=1, keepdims=True)
    rate_c = jnp.sum(jnp.where(eye, code[...].astype(f32), 0.0), axis=1, keepdims=True) / (256.0 * full_length)

    if gather:
        for r in range(1, n_dp):
            w_copy(r, lax.rem(dp + r, n_dp), lax.rem(dp - r + n_dp, n_dp)).wait_recv()
    proj = jnp.zeros((heads, length), f32)
    for d in range(n_dp):
        proj = proj + mm_nt(wall[d] if gather else w[d], hid[:, d * depth:(d + 1) * depth])
    shifted = proj + bias_c
    timestep = jnp.maximum(shifted, 0.0) + jnp.log1p(jnp.exp(-jnp.abs(shifted)))
    gain = 1.0 / (1.0 + jnp.exp(-shifted))
    rows = lax.broadcasted_iota(jnp.int32, (length, length), 0)
    cols = lax.broadcasted_iota(jnp.int32, (length, length), 1)
    causal = rows <= cols
    cum = jnp.dot(-rate_c * timestep, causal.astype(f32), precision=exact, preferred_element_type=f32)
    last = jnp.broadcast_to(cum[:, length - 1:length], (heads, length))
    cum_s[...] = cum
    last_s[...] = last
    growth_s[...] = jnp.exp(cum)
    elast_s[...] = jnp.exp(last)

    def chain(k):
        span = pl.ds(pl.multiple_of(k * (CHUNK_HEADS * HEADDIM), CHUNK_HEADS * HEADDIM), CHUNK_HEADS * HEADDIM)
        return pltpu.make_async_remote_copy(
            src_ref=send_s.at[span], dst_ref=recv_s.at[span], send_sem=ch_send.at[k], recv_sem=ch_recv.at[k],
            device_id=(dp, lax.rem(ctx - 1 + n_ctx, n_ctx)), device_id_type=MESH)

    def own_chunk(k, carry):
        for e in range(CHUNK_HEADS):
            h = k * CHUNK_HEADS + e
            span = pl.ds(pl.multiple_of(h * HEADDIM, HEADDIM), HEADDIM)
            weighted = cot_t[span, :].astype(f32) * growth_s[pl.ds(h, 1), :]
            both = mm(jnp.concatenate(split(weighted), axis=0), cg2[hg[h], :length, :])
            send_s[span, :] = both[:HEADDIM] + both[HEADDIM:]

        @pl.when(is_last)
        def _():
            chain(k).start()

        return carry

    chunks = heads // CHUNK_HEADS
    lax.fori_loop(0, chunks, own_chunk, 0)

    both_t = jnp.concatenate([cum, timestep, jnp.zeros((length - 2 * heads, length), f32)], axis=0).T
    for h in range(heads):
        cumb[h] = jnp.broadcast_to(both_t[:, h:h + 1], (length, length))
        stepb[h] = jnp.broadcast_to(both_t[:, heads + h:heads + h + 1], (length, length))

    low_lanes = lax.broadcasted_iota(jnp.int32, (length, 128), 1) < HEADDIM
    ones = jnp.ones((8, 256), bf16)

    def main_chunk(k, carry):
        @pl.when(ctx < n_ctx - 1)
        def _():
            chain(k).wait_recv()

        @pl.when(jnp.logical_and(ctx < n_ctx - 1, ctx > 0))
        def _():
            for e in range(CHUNK_HEADS):
                h = k * CHUNK_HEADS + e
                span = pl.ds(pl.multiple_of(h * HEADDIM, HEADDIM), HEADDIM)
                send_s[span, :] = send_s[span, :] + elast_s[pl.ds(h, 1), :] * recv_s[span, :]
            chain(k).start()

        grads = []
        for q in range(CHUNK_HEADS // 2):
            pair = k * (CHUNK_HEADS // 2) + q
            lanes = pl.ds(pl.multiple_of(pair * 128, 128), 128)
            xp = x[:, lanes]
            cp = cot[:, lanes]
            incoming = recv_s[lanes, :]
            rhs = jnp.concatenate(split(incoming), axis=0)
            product_state = incoming * st[lanes, :].astype(f32)
            for e in range(2):
                h = pair * 2 + e
                g = hg[h]
                row = pl.ds(h, 1)
                span = pl.ds(pl.multiple_of(h * HEADDIM, HEADDIM), HEADDIM)
                mask = low_lanes if e == 0 else jnp.logical_not(low_lanes)
                xm = jnp.where(mask, xp, jnp.zeros_like(xp))
                c2 = cg2[g]
                cum_h = cumb[h]
                step_h = stepb[h]
                gaps = cum_s[row, :] - cum_h
                decay = jnp.where(causal, jnp.exp(jnp.where(causal, gaps, 0.0)), 0.0)
                m = decay * mm_nt(xm, cp)
                scored = m * sc[g]
                x_state = mm(jnp.concatenate([xm, xm], axis=1), rhs)
                to_end = jnp.exp(last_s[row, :] - cum_h)
                grads.append((h, step_h * (mm(jnp.concatenate(split(m), axis=1), c2) + to_end * x_state)))
                row_s[row, :] = jnp.sum(scored * step_h, axis=0, keepdims=True)
                col_s[row, :] = mm_nt(ones, jnp.concatenate(split(scored), axis=1))[:1]
                end_s[row, :] = mm_nt(ones, jnp.concatenate(split(x_state * bg[g]), axis=1))[:1]
                carried = mm_nt(st[span, :], c2[:length])
                car_s[row, :] = jnp.sum(cot_t[span, :].astype(f32) * carried, axis=0, keepdims=True)
                gs_s[row, :] = jnp.sum(
                    product_state[e * HEADDIM:(e + 1) * HEADDIM], axis=0, keepdims=True)
        for g in range(GROUPS):
            total = acc[g]
            for h, value in grads:
                total = total + jnp.where(hg[h] == g, 1.0, 0.0) * value
            acc[g] = total
        return carry

    lax.fori_loop(0, chunks, main_chunk, 0)

    col = col_s[...]
    end_plain = jnp.exp(last_s[...] - cum_s[...]) * end_s[...]
    end_term = end_plain * timestep
    grad_cum = row_s[...] - col * timestep + growth_s[...] * car_s[...] - end_term
    end_total = jnp.sum(end_term, axis=1, keepdims=True) + elast_s[:, :1] * jnp.sum(gs_s[...], axis=1, keepdims=True)
    lane = lax.broadcasted_iota(jnp.int32, (heads, length), 1)
    grad_cum = grad_cum + jnp.where(lane == length - 1, end_total, 0.0)
    backward = jnp.dot(grad_cum, (rows >= cols).astype(f32), precision=exact, preferred_element_type=f32)
    grad_raw = (col + end_plain - rate_c * backward) * gain

    def g_copy(r, peer, slot):
        return pltpu.make_async_remote_copy(
            src_ref=graw_own, dst_ref=graw_all.at[slot], send_sem=g_send.at[r], recv_sem=g_recv.at[r],
            device_id=(peer, ctx), device_id_type=MESH)

    def p_copy(r, peer, slot):
        return pltpu.make_async_remote_copy(
            src_ref=part, dst_ref=p_all.at[slot], send_sem=p_send.at[r], recv_sem=p_recv.at[r],
            device_id=(dp, peer), device_id_type=MESH)

    if fuse:
        graw_own[...] = grad_raw
        for r in range(1, n_dp):
            g_copy(r, lax.rem(dp + r, n_dp), dp).start()
        graw_all[dp] = grad_raw
    else:
        out_w[...] = grad_raw

    for g in range(GROUPS):
        out_b[:, pl.ds(NSTATE * g, NSTATE)] = acc[g].astype(bf16)

    if fuse:
        total = jnp.zeros((2 * heads, depth), f32)
        for r in range(1, n_dp):
            source = lax.rem(dp - r + n_dp, n_dp)
            h_copy(r, lax.rem(dp + r, n_dp), source).wait_recv()
        for r in range(1, n_dp):
            source = lax.rem(dp - r + n_dp, n_dp)
            g_copy(r, lax.rem(dp + r, n_dp), source).wait_recv()
        for d in range(n_dp):
            total = total + mm(jnp.concatenate(split(graw_all[d]), axis=0), hall[d])
        part[...] = total[:heads] + total[heads:]
        for r in range(1, n_ctx):
            p_copy(r, lax.rem(ctx + r, n_ctx), ctx).start()
        p_all[ctx] = part[...]
        for r in range(1, n_ctx):
            p_copy(r, lax.rem(ctx + r, n_ctx), lax.rem(ctx - r + n_ctx, n_ctx)).wait_recv()
        summed = p_all[0]
        for d in range(1, n_ctx):
            summed = summed + p_all[d]
        out_w[...] = summed
        for r in range(1, n_ctx):
            p_copy(r, lax.rem(ctx + r, n_ctx), ctx).wait_send()
        for r in range(1, n_dp):
            h_copy(r, lax.rem(dp + r, n_dp), dp).wait_send()
            g_copy(r, lax.rem(dp + r, n_dp), dp).wait_send()

    if gather:
        for r in range(1, n_dp):
            w_copy(r, lax.rem(dp + r, n_dp), dp).wait_send()

    @pl.when(ctx > 0)
    def _():
        def drain(k, carry):
            chain(k).wait_send()
            return carry

        lax.fori_loop(0, chunks, drain, 0)


def body(n_dp, n_ctx, hidden, dt_weight, ssm_input, grad_output, b_matrix, c_matrix,
         stored_states, step_bias, decay_code, head_group):
    length, width = hidden.shape[1:]
    depth = dt_weight.shape[0]
    heads = step_bias.shape[0]
    gather = depth % 128 == 0
    fuse = FUSE_END and gather
    hid = hidden[0]
    if gather:
        w = dt_weight
    else:
        w = lax.all_gather(dt_weight.T, "dp", axis=0, tiled=False)
    chunks = heads // CHUNK_HEADS
    vmem = pl.BlockSpec(memory_space=pltpu.VMEM)
    small = pltpu.VMEM((heads, length), f32)
    dma = pltpu.SemaphoreType.DMA
    scratch = [
        pltpu.VMEM((n_dp if gather else 1, heads, depth), bf16),
        pltpu.VMEM((heads * HEADDIM, length), bf16),
        pltpu.VMEM((GROUPS, length, NSTATE), f32),
        pltpu.VMEM((GROUPS, 2 * length, NSTATE), bf16),
        pltpu.VMEM((GROUPS, length, length), f32),
        small, small, small, small,
        pltpu.VMEM((heads, length, length), f32),
        pltpu.VMEM((heads, length, length), f32),
        pltpu.VMEM((GROUPS, length, NSTATE), f32),
        small, small, small, small, small,
        pltpu.VMEM((heads * HEADDIM, NSTATE), f32),
        pltpu.VMEM((heads * HEADDIM, NSTATE), f32),
        pltpu.VMEM((heads, depth), bf16),
        dma((n_dp,)), dma((n_dp,)), dma((chunks,)), dma((chunks,)),
    ]
    if fuse:
        scratch += [
            pltpu.VMEM((n_dp, length, depth), bf16),
            small,
            pltpu.VMEM((n_dp, heads, length), f32),
            pltpu.VMEM((heads, depth), f32),
            dma((n_dp,)), dma((n_dp,)), dma((n_dp,)), dma((n_dp,)),
            pltpu.VMEM((n_ctx, heads, depth), f32),
            dma((n_ctx,)), dma((n_ctx,)),
        ]
    grad_b, res = pl.pallas_call(
        functools.partial(kernel, (n_dp, n_ctx, gather, fuse)),
        out_shape=(
            jax.ShapeDtypeStruct((length, GROUPS * NSTATE), bf16),
            jax.ShapeDtypeStruct((heads, depth if fuse else length), f32),
        ),
        in_specs=[vmem] * 9 + [pl.BlockSpec(memory_space=pltpu.SMEM)],
        out_specs=(vmem, vmem),
        scratch_shapes=scratch,
        compiler_params=pltpu.CompilerParams(
            collective_id=0, has_side_effects=True, vmem_limit_bytes=48 * 1024 * 1024),
    )(hid, w, ssm_input[0], grad_output[0], b_matrix[0], c_matrix[0],
      stored_states.reshape(heads * HEADDIM, NSTATE), step_bias.reshape(1, heads),
      decay_code.reshape(1, heads), head_group)
    if fuse:
        grad_w = res.T
    else:
        hi = lax.reduce_precision(res, 8, 7)
        both = mm(jnp.concatenate([hi.astype(bf16), (res - hi).astype(bf16)], axis=0), hid)
        part = both[:heads] + both[heads:]
        part = lax.psum_scatter(part, "dp", scatter_dimension=1, tiled=True)
        grad_w = lax.psum(part, "ctx").T
    return grad_b[None], grad_w


def solution(mesh):
    return jax.shard_map(
        functools.partial(body, mesh.shape["dp"], mesh.shape["ctx"]),
        mesh=mesh,
        in_specs=(
            P("dp", "ctx", None),
            P("dp", None),
            P("dp", "ctx", None),
            P("dp", "ctx", None),
            P("dp", "ctx", None),
            P("dp", "ctx", None),
            P("dp", "ctx", None, None, None),
            P(),
            P(),
            P(),
        ),
        out_specs=(P("dp", "ctx", None), P("dp", None)),
        check_vma=False,
    )
```

profile of v0, /device:TPU:0, one launch (start us, length us, event | category | flops | bytes accessed | tf_op | source)
XLA Modules:
  0.0 69.6 jit_solution(7170300777369258059)
XLA Ops:
  0.6 0.0 copy-start.6
  0.6 0.0 copy-start.7
  0.7 0.0 copy-start.8
  0.7 0.9 %copy.12.w = bf16[512,32]{1,0:T(8,128)(2,1)S(1)} copy(bf16[512,32]{0,1:T(8,128)(2,1)} %param.11) | data formatting | bytes 65536 | tf_op args[1]
  1.6 0.0 copy-done.6
  1.6 0.0 copy-done.7
  1.6 0.0 copy-done.8
  1.6 0.0 copy-start
  1.6 1.2 %copy-done = bf16[1,128,4096]{2,1,0:T(8,128)(2,1)S(1)} copy-done((bf16[1,128,4096]{2,1,0:T(8,128)(2,1)S(1)}, bf16[1,128,4096]{2,1,0:T(8,128)(2,1)}, u32[]{:S(2)}) %copy-start) | copy-done | bytes 1048600
  2.8 0.0 copy-start.1
  2.8 1.0 %copy-done.1 = bf16[1,128,2048]{2,1,0:T(8,128)(2,1)S(1)} copy-done((bf16[1,128,2048]{2,1,0:T(8,128)(2,1)S(1)}, bf16[1,128,2048]{2,1,0:T(8,128)(2,1)}, u32[]{:S(2)}) %copy-start.1) | copy-done | bytes 524312
  3.9 0.0 copy-start.2
  3.9 1.0 %copy-done.2 = bf16[1,128,2048]{2,1,0:T(8,128)(2,1)S(1)} copy-done((bf16[1,128,2048]{2,1,0:T(8,128)(2,1)S(1)}, bf16[1,128,2048]{2,1,0:T(8,128)(2,1)}, u32[]{:S(2)}) %copy-start.2) | copy-done | bytes 524312
  4.9 0.0 copy-start.3
  4.9 1.0 %copy-done.3 = bf16[1,1,32,64,128]{4,3,2,1,0:T(8,128)(2,1)S(1)} copy-done((bf16[1,1,32,64,128]{4,3,2,1,0:T(8,128)(2,1)S(1)}, bf16[1,1,32,64,128]{4,3,2,1,0:T(8,128)(2,1)}, u32[]{:S(2)}) %copy-start.3) | copy-done | bytes 524312
  5.9 0.0 copy-start.4
  5.9 0.9 %copy-done.4 = bf16[1,128,1024]{2,1,0:T(8,128)(2,1)S(1)} copy-done((bf16[1,128,1024]{2,1,0:T(8,128)(2,1)S(1)}, bf16[1,128,1024]{2,1,0:T(8,128)(2,1)}, u32[]{:S(2)}) %copy-start.4) | copy-done | bytes 262168
  6.9 0.0 copy-start.5
  6.9 0.9 %copy-done.5 = bf16[1,128,1024]{2,1,0:T(8,128)(2,1)S(1)} copy-done((bf16[1,128,1024]{2,1,0:T(8,128)(2,1)S(1)}, bf16[1,128,1024]{2,1,0:T(8,128)(2,1)}, u32[]{:S(2)}) %copy-start.5) | copy-done | bytes 262168
  7.8 60.4 %shard_map.113 = (bf16[128,1024]{1,0:T(8,128)(2,1)S(1)}, f32[32,512]{1,0:T(8,128)S(1)}) custom-call(bf16[128,4096]{1,0:T(8,128)(2,1)S(1)} %bitcast.10, bf16[512,32]{1,0:T(8,128)(2,1)S(1)} %copy.12.w, bf16[128,2048]{1,0:T(8,128)(2,1)S(1)} %bitcast.11, bf16[128,2048]{1,0:T(8,128)(2,1)S(1)} %bitcast.12, bf16[128,1024]{1,0:T(8,128)(2,1)S(1)} %bitcast.14, ...), custom_call_target="tpu_custom_call" | custom-call | tf_op jit(solution)/shard_map/pallas_call | solution.py:319
  68.3 0.7 %copy.15 = bf16[1,128,1024]{2,1,0:T(8,128)(2,1)} copy(bf16[1,128,1024]{2,1,0:T(8,128)(2,1)S(1)} %bitcast.16) | data formatting | bytes 524288
  69.0 0.6 copy.16
Async XLA Ops:
  0.6 0.9 %copy-start.6 = (f32[32]{0:T(128)S(1)}, f32[32]{0:T(128)}, u32[]{:S(2)}) copy-start(f32[32]{0:T(128)} %param.17) | copy-start | bytes 388
  0.6 0.9 %copy-start.7 = (s32[32]{0:T(128)S(1)}, s32[32]{0:T(128)}, u32[]{:S(2)}) copy-start(s32[32]{0:T(128)} %param.18) | copy-start | bytes 388
  0.7 0.9 %copy-start.8 = (s32[32]{0:T(128)S(1)}, s32[32]{0:T(128)}, u32[]{:S(2)}) copy-start(s32[32]{0:T(128)} %hg.1) | copy-start | bytes 388
  1.6 1.2 %copy-start = (bf16[1,128,4096]{2,1,0:T(8,128)(2,1)S(1)}, bf16[1,128,4096]{2,1,0:T(8,128)(2,1)}, u32[]{:S(2)}) copy-start(bf16[1,128,4096]{2,1,0:T(8,128)(2,1)} %param.10) | copy-start | bytes 3145732
  2.8 1.0 %copy-start.1 = (bf16[1,128,2048]{2,1,0:T(8,128)(2,1)S(1)}, bf16[1,128,2048]{2,1,0:T(8,128)(2,1)}, u32[]{:S(2)}) copy-start(bf16[1,128,2048]{2,1,0:T(8,128)(2,1)} %param.12) | copy-start | bytes 1572868
  3.9 1.0 %copy-start.2 = (bf16[1,128,2048]{2,1,0:T(8,128)(2,1)S(1)}, bf16[1,128,2048]{2,1,0:T(8,128)(2,1)}, u32[]{:S(2)}) copy-start(bf16[1,128,2048]{2,1,0:T(8,128)(2,1)} %param.13) | copy-start | bytes 1572868
  4.9 1.0 %copy-start.3 = (bf16[1,1,32,64,128]{4,3,2,1,0:T(8,128)(2,1)S(1)}, bf16[1,1,32,64,128]{4,3,2,1,0:T(8,128)(2,1)}, u32[]{:S(2)}) copy-start(bf16[1,1,32,64,128]{4,3,2,1,0:T(8,128)(2,1)} %param.16) | copy-start | bytes 1572868
  5.9 0.9 %copy-start.4 = (bf16[1,128,1024]{2,1,0:T(8,128)(2,1)S(1)}, bf16[1,128,1024]{2,1,0:T(8,128)(2,1)}, u32[]{:S(2)}) copy-start(bf16[1,128,1024]{2,1,0:T(8,128)(2,1)} %param.14) | copy-start | bytes 786436
  6.9 0.9 %copy-start.5 = (bf16[1,128,1024]{2,1,0:T(8,128)(2,1)S(1)}, bf16[1,128,1024]{2,1,0:T(8,128)(2,1)}, u32[]{:S(2)}) copy-start(bf16[1,128,1024]{2,1,0:T(8,128)(2,1)} %param.15) | copy-start | bytes 786436
where the time goes:
time: 70 us; the launch traced here: 69.6 us
  Pallas kernels  60.4 us (86%)
  local copies, waits for them, and re-layouts  8.48 us (12%)
    pallas_call x1, Pallas kernels, body(): pl.pallas_call(functools.partial(kernel, (n_dp, n_ctx, gather, fuse)), ou...  60.4 us
    unnamed x21, local copies, waits for them, and re-layouts  8.48 us

commit v1 on v0

--- a/solution.py
+++ b/solution.py
@@ -31,12 +31,12 @@
     return hi, (v - hi.astype(f32)).astype(bf16)
 
 
-def kernel(cfg, hid, w, x, cot, b, c, st, bias, code, hg, *rest):
+def kernel(cfg, hid_h, w, x_h, cot_h, b_h, c_h, st_h, bias, code, hg, *rest):
     n_dp, n_ctx, gather, fuse = cfg
     (out_b, out_w), rest = rest[:2], rest[2:]
     (wall, cot_t, bg, cg2, sc, cum_s, last_s, growth_s, elast_s, cumb, stepb, acc,
-     row_s, col_s, car_s, end_s, gs_s, send_s, recv_s, w_own,
-     w_send, w_recv, ch_send, ch_recv) = rest[:24]
+     row_s, col_s, car_s, end_s, gs_s, send_s, recv_s, hid, x, cot, b, c, st, in_sem,
+     w_send, w_recv, ch_send, ch_recv) = rest[:30]
     length = x.shape[0]
     heads = bias.shape[1]
     depth = hid.shape[1] // n_dp
@@ -46,8 +46,14 @@
     is_last = ctx == n_ctx - 1
 
     if fuse:
-        hall, graw_own, graw_all, part, h_send, h_recv, g_send, g_recv, p_all, p_send, p_recv = rest[24:]
-
+        hall, graw_own, graw_all, part, h_send, h_recv, g_send, g_recv, p_all, p_send, p_recv = rest[30:]
+
+    fetches = [
+        pltpu.make_async_copy(source, target, in_sem.at[i])
+        for i, (source, target) in enumerate(
+            ((cot_h, cot), (c_h, c), (b_h, b), (hid_h, hid), (x_h, x), (st_h, st)))
+    ]
+    own_w = pltpu.make_async_copy(w, wall.at[dp if gather else 0], in_sem.at[6])
     barrier = pltpu.get_barrier_semaphore()
     if gather or fuse:
         for r in range(1, n_dp):
@@ -59,30 +65,33 @@
     ci = lax.broadcasted_iota(jnp.int32, (heads, heads), 1)
     eye = ri == ci
     if gather:
-        w_own[...] = mm_nt(eye.astype(bf16), w[...]).astype(bf16)
+        own_w.start()
+    for fetch in fetches:
+        fetch.start()
     pl.semaphore_wait(barrier, (n_dp - 1 if gather or fuse else 0) + n_ctx - 1)
 
     def w_copy(r, peer, slot):
         return pltpu.make_async_remote_copy(
-            src_ref=w_own, dst_ref=wall.at[slot], send_sem=w_send.at[r], recv_sem=w_recv.at[r],
+            src_ref=w, dst_ref=wall.at[slot], send_sem=w_send.at[r], recv_sem=w_recv.at[r],
             device_id=(peer, ctx), device_id_type=MESH)
 
     def h_copy(r, peer, slot):
         return pltpu.make_async_remote_copy(
-            src_ref=hid.at[:, pl.ds(pl.multiple_of(peer * depth, depth), depth)], dst_ref=hall.at[slot],
+            src_ref=hid_h.at[:, pl.ds(pl.multiple_of(peer * depth, depth), depth)], dst_ref=hall.at[slot],
             send_sem=h_send.at[r], recv_sem=h_recv.at[r], device_id=(peer, ctx), device_id_type=MESH)
 
     if gather:
         for r in range(1, n_dp):
             w_copy(r, lax.rem(dp + r, n_dp), dp).start()
-        wall[dp] = w_own[...]
     if fuse:
         for r in range(1, n_dp):
             h_copy(r, lax.rem(dp + r, n_dp), dp).start()
-        hall[dp] = hid[:, pl.ds(pl.multiple_of(dp * depth, depth), depth)]
-
+
+    fetches[0].wait()
     for k in range(x.shape[1] // 128):
         cot_t[pl.ds(128 * k, 128), :] = cot[:, pl.ds(128 * k, 128)].T
+    fetches[1].wait()
+    fetches[2].wait()
     for g in range(GROUPS):
         b_g = b[:, pl.ds(NSTATE * g, NSTATE)]
         c_g = c[:, pl.ds(NSTATE * g, NSTATE)]
@@ -99,7 +108,11 @@
     bias_c = jnp.sum(jnp.where(eye, bias[...], 0.0), axis=1, keepdims=True)
     rate_c = jnp.sum(jnp.where(eye, code[...].astype(f32), 0.0), axis=1, keepdims=True) / (256.0 * full_length)
 
-    if gather:
+    fetches[3].wait()
+    if fuse:
+        hall[dp] = hid[:, pl.ds(pl.multiple_of(dp * depth, depth), depth)]
+    if gather:
+        own_w.wait()
         for r in range(1, n_dp):
             w_copy(r, lax.rem(dp + r, n_dp), lax.rem(dp - r + n_dp, n_dp)).wait_recv()
     proj = jnp.zeros((heads, length), f32)
@@ -202,6 +215,8 @@
             acc[g] = total
         return carry
 
+    fetches[4].wait()
+    fetches[5].wait()
     lax.fori_loop(0, chunks, main_chunk, 0)
 
     col = col_s[...]
@@ -283,10 +298,11 @@
     fuse = FUSE_END and gather
     hid = hidden[0]
     if gather:
-        w = dt_weight
+        w = dt_weight.T
     else:
         w = lax.all_gather(dt_weight.T, "dp", axis=0, tiled=False)
     chunks = heads // CHUNK_HEADS
+    any_ = pl.BlockSpec(memory_space=pl.ANY)
     vmem = pl.BlockSpec(memory_space=pltpu.VMEM)
     small = pltpu.VMEM((heads, length), f32)
     dma = pltpu.SemaphoreType.DMA
@@ -303,7 +319,13 @@
         small, small, small, small, small,
         pltpu.VMEM((heads * HEADDIM, NSTATE), f32),
         pltpu.VMEM((heads * HEADDIM, NSTATE), f32),
-        pltpu.VMEM((heads, depth), bf16),
+        pltpu.VMEM(hid.shape, bf16),
+        pltpu.VMEM(ssm_input.shape[1:], bf16),
+        pltpu.VMEM(grad_output.shape[1:], bf16),
+        pltpu.VMEM(b_matrix.shape[1:], bf16),
+        pltpu.VMEM(c_matrix.shape[1:], bf16),
+        pltpu.VMEM((heads * HEADDIM, NSTATE), bf16),
+        dma((7,)),
         dma((n_dp,)), dma((n_dp,)), dma((chunks,)), dma((chunks,)),
     ]
     if fuse:
@@ -322,7 +344,7 @@
             jax.ShapeDtypeStruct((length, GROUPS * NSTATE), bf16),
             jax.ShapeDtypeStruct((heads, depth if fuse else length), f32),
         ),
-        in_specs=[vmem] * 9 + [pl.BlockSpec(memory_space=pltpu.SMEM)],
+        in_specs=[any_] + [any_ if gather else vmem] + [any_] * 5 + [vmem] * 2 + [pl.BlockSpec(memory_space=pltpu.SMEM)],
         out_specs=(vmem, vmem),
         scratch_shapes=scratch,
         compiler_params=pltpu.CompilerParams(

time: 70 us -> 70.6 us (level)
    unnamed x21 -> x22, local copies, waits for them, and re-layouts: 8.48 us -> 9 us
where the time goes in v1:
time: 70.6 us; the launch traced here: 70.1 us
  Pallas kernels  60.5 us (86%)
  local copies, waits for them, and re-layouts  9 us (13%)
    pallas_call x1, Pallas kernels, body(): pl.pallas_call(functools.partial(kernel, (n_dp, n_ctx, gather, fuse)), ou...  60.5 us
    unnamed x22, local copies, waits for them, and re-layouts  9 us

profile of v1, /device:TPU:0, one launch (start us, length us, event | category | flops | bytes accessed | tf_op | source)
XLA Modules:
  0.0 70.1 jit_solution(9653095796909147315)
XLA Ops:
  0.6 0.0 copy-start.7
  0.6 0.0 copy-start.8
  0.7 0.0 copy-start.9
  0.7 0.6 copy-done.7
  1.3 0.0 copy-done.8
  1.3 0.0 copy-done.9
  1.3 0.0 copy-start
  1.3 1.2 %copy-done = bf16[1,128,4096]{2,1,0:T(8,128)(2,1)S(1)} copy-done((bf16[1,128,4096]{2,1,0:T(8,128)(2,1)S(1)}, bf16[1,128,4096]{2,1,0:T(8,128)(2,1)}, u32[]{:S(2)}) %copy-start) | copy-done | bytes 1048600
  2.5 0.0 copy-start.1
  2.5 1.0 %copy-done.1 = bf16[1,128,2048]{2,1,0:T(8,128)(2,1)S(1)} copy-done((bf16[1,128,2048]{2,1,0:T(8,128)(2,1)S(1)}, bf16[1,128,2048]{2,1,0:T(8,128)(2,1)}, u32[]{:S(2)}) %copy-start.1) | copy-done | bytes 524312
  3.6 0.0 copy-start.2
  3.6 1.0 %copy-done.2 = bf16[1,128,2048]{2,1,0:T(8,128)(2,1)S(1)} copy-done((bf16[1,128,2048]{2,1,0:T(8,128)(2,1)S(1)}, bf16[1,128,2048]{2,1,0:T(8,128)(2,1)}, u32[]{:S(2)}) %copy-start.2) | copy-done | bytes 524312
  4.6 0.0 copy-start.3
  4.6 1.0 %copy-done.3 = bf16[1,1,32,64,128]{4,3,2,1,0:T(8,128)(2,1)S(1)} copy-done((bf16[1,1,32,64,128]{4,3,2,1,0:T(8,128)(2,1)S(1)}, bf16[1,1,32,64,128]{4,3,2,1,0:T(8,128)(2,1)}, u32[]{:S(2)}) %copy-start.3) | copy-done | bytes 524312
  5.7 0.0 copy-start.4
  5.7 0.9 %copy-done.4 = bf16[1,128,1024]{2,1,0:T(8,128)(2,1)S(1)} copy-done((bf16[1,128,1024]{2,1,0:T(8,128)(2,1)S(1)}, bf16[1,128,1024]{2,1,0:T(8,128)(2,1)}, u32[]{:S(2)}) %copy-start.4) | copy-done | bytes 262168
  6.6 0.0 copy-start.5
  6.6 0.9 %copy-done.5 = bf16[1,128,1024]{2,1,0:T(8,128)(2,1)S(1)} copy-done((bf16[1,128,1024]{2,1,0:T(8,128)(2,1)S(1)}, bf16[1,128,1024]{2,1,0:T(8,128)(2,1)}, u32[]{:S(2)}) %copy-start.5) | copy-done | bytes 262168
  7.6 0.0 copy-start.6
  7.6 0.8 %copy-done.6 = bf16[512,32]{0,1:T(8,128)(2,1)S(1)} copy-done((bf16[512,32]{0,1:T(8,128)(2,1)S(1)}, bf16[512,32]{0,1:T(8,128)(2,1)}, u32[]{:S(2)}) %copy-start.6) | copy-done | bytes 32792
  8.3 60.5 %shard_map.113 = (bf16[128,1024]{1,0:T(8,128)(2,1)S(1)}, f32[32,512]{1,0:T(8,128)S(1)}) custom-call(bf16[128,4096]{1,0:T(8,128)(2,1)S(1)} %bitcast.11, bf16[32,512]{1,0:T(8,128)(2,1)S(1)} %bitcast.19, bf16[128,2048]{1,0:T(8,128)(2,1)S(1)} %bitcast.12, bf16[128,2048]{1,0:T(8,128)(2,1)S(1)} %bitcast.13, bf16[128,1024]{1,0:T(8,128)(2,1)S(1)} %bitcast.15, ...), custom_call_target="tpu_custom_call" | custom-call | tf_op jit(solution)/shard_map/pallas_call | solution.py:341
  68.8 0.7 %copy.14 = bf16[1,128,1024]{2,1,0:T(8,128)(2,1)} copy(bf16[1,128,1024]{2,1,0:T(8,128)(2,1)S(1)} %bitcast.17) | data formatting | bytes 524288
  69.5 0.6 copy.15
Async XLA Ops:
  0.6 0.7 copy-start.7
  0.6 0.7 copy-start.8
  0.7 0.7 copy-start.9
  1.3 1.2 %copy-start = (bf16[1,128,4096]{2,1,0:T(8,128)(2,1)S(1)}, bf16[1,128,4096]{2,1,0:T(8,128)(2,1)}, u32[]{:S(2)}) copy-start(bf16[1,128,4096]{2,1,0:T(8,128)(2,1)} %param.10) | copy-start | bytes 3145732
  2.5 1.0 %copy-start.1 = (bf16[1,128,2048]{2,1,0:T(8,128)(2,1)S(1)}, bf16[1,128,2048]{2,1,0:T(8,128)(2,1)}, u32[]{:S(2)}) copy-start(bf16[1,128,2048]{2,1,0:T(8,128)(2,1)} %param.12) | copy-start | bytes 1572868
  3.6 1.0 %copy-start.2 = (bf16[1,128,2048]{2,1,0:T(8,128)(2,1)S(1)}, bf16[1,128,2048]{2,1,0:T(8,128)(2,1)}, u32[]{:S(2)}) copy-start(bf16[1,128,2048]{2,1,0:T(8,128)(2,1)} %param.13) | copy-start | bytes 1572868
  4.6 1.0 %copy-start.3 = (bf16[1,1,32,64,128]{4,3,2,1,0:T(8,128)(2,1)S(1)}, bf16[1,1,32,64,128]{4,3,2,1,0:T(8,128)(2,1)}, u32[]{:S(2)}) copy-start(bf16[1,1,32,64,128]{4,3,2,1,0:T(8,128)(2,1)} %param.16) | copy-start | bytes 1572868
  5.7 0.9 %copy-start.4 = (bf16[1,128,1024]{2,1,0:T(8,128)(2,1)S(1)}, bf16[1,128,1024]{2,1,0:T(8,128)(2,1)}, u32[]{:S(2)}) copy-start(bf16[1,128,1024]{2,1,0:T(8,128)(2,1)} %param.14) | copy-start | bytes 786436
  6.6 0.9 %copy-start.5 = (bf16[1,128,1024]{2,1,0:T(8,128)(2,1)S(1)}, bf16[1,128,1024]{2,1,0:T(8,128)(2,1)}, u32[]{:S(2)}) copy-start(bf16[1,128,1024]{2,1,0:T(8,128)(2,1)} %param.15) | copy-start | bytes 786436
  7.6 0.8 %copy-start.6 = (bf16[512,32]{0,1:T(8,128)(2,1)S(1)}, bf16[512,32]{0,1:T(8,128)(2,1)}, u32[]{:S(2)}) copy-start(bf16[512,32]{0,1:T(8,128)(2,1)} %param.11) | copy-start | bytes 98308

commit v2 on v1

--- a/solution.py
+++ b/solution.py
@@ -10,7 +10,7 @@
 HEADDIM = 64
 NSTATE = 128
 GROUPS = 8
-CHUNK_HEADS = 4
+CHUNK_HEADS = 2
 FUSE_END = True
 
 f32, bf16 = jnp.float32, jnp.bfloat16
@@ -302,7 +302,7 @@
     else:
         w = lax.all_gather(dt_weight.T, "dp", axis=0, tiled=False)
     chunks = heads // CHUNK_HEADS
-    any_ = pl.BlockSpec(memory_space=pl.ANY)
+    any_ = pl.BlockSpec(memory_space=pltpu.HBM)
     vmem = pl.BlockSpec(memory_space=pltpu.VMEM)
     small = pltpu.VMEM((heads, length), f32)
     dma = pltpu.SemaphoreType.DMA

time: 70.6 us -> 68.5 us (0.970)
  Pallas kernels: 60.5 us -> 58.3 us
    pallas_call x1, Pallas kernels: 60.5 us -> 58.3 us  [body(): pl.pallas_call(functools.partial(kernel, (n_dp, n_ctx, gather, fuse)), ou...]
where the time goes in v2:
time: 68.5 us; the launch traced here: 68 us
  Pallas kernels  58.3 us (85%)
  local copies, waits for them, and re-layouts  9 us (13%)
    pallas_call x1, Pallas kernels, body(): pl.pallas_call(functools.partial(kernel, (n_dp, n_ctx, gather, fuse)), ou...  58.3 us
    unnamed x22, local copies, waits for them, and re-layouts  9 us

profile of v2, /device:TPU:0, one launch (start us, length us, event | category | flops | bytes accessed | tf_op | source)
XLA Modules:
  0.0 68.0 jit_solution(1446761835052112054)
XLA Ops:
  0.6 0.0 copy-start.7
  0.6 0.0 copy-start.8
  0.7 0.0 copy-start.9
  0.7 0.6 copy-done.7
  1.3 0.0 copy-done.8
  1.3 0.0 copy-done.9
  1.3 0.0 copy-start
  1.3 1.2 %copy-done = bf16[1,128,4096]{2,1,0:T(8,128)(2,1)S(1)} copy-done((bf16[1,128,4096]{2,1,0:T(8,128)(2,1)S(1)}, bf16[1,128,4096]{2,1,0:T(8,128)(2,1)}, u32[]{:S(2)}) %copy-start) | copy-done | bytes 1048600
  2.5 0.0 copy-start.1
  2.5 1.0 %copy-done.1 = bf16[1,128,2048]{2,1,0:T(8,128)(2,1)S(1)} copy-done((bf16[1,128,2048]{2,1,0:T(8,128)(2,1)S(1)}, bf16[1,128,2048]{2,1,0:T(8,128)(2,1)}, u32[]{:S(2)}) %copy-start.1) | copy-done | bytes 524312
  3.6 0.0 copy-start.2
  3.6 1.0 %copy-done.2 = bf16[1,128,2048]{2,1,0:T(8,128)(2,1)S(1)} copy-done((bf16[1,128,2048]{2,1,0:T(8,128)(2,1)S(1)}, bf16[1,128,2048]{2,1,0:T(8,128)(2,1)}, u32[]{:S(2)}) %copy-start.2) | copy-done | bytes 524312
  4.6 0.0 copy-start.3
  4.6 1.0 %copy-done.3 = bf16[1,1,32,64,128]{4,3,2,1,0:T(8,128)(2,1)S(1)} copy-done((bf16[1,1,32,64,128]{4,3,2,1,0:T(8,128)(2,1)S(1)}, bf16[1,1,32,64,128]{4,3,2,1,0:T(8,128)(2,1)}, u32[]{:S(2)}) %copy-start.3) | copy-done | bytes 524312
  5.7 0.0 copy-start.4
  5.7 0.9 %copy-done.4 = bf16[1,128,1024]{2,1,0:T(8,128)(2,1)S(1)} copy-done((bf16[1,128,1024]{2,1,0:T(8,128)(2,1)S(1)}, bf16[1,128,1024]{2,1,0:T(8,128)(2,1)}, u32[]{:S(2)}) %copy-start.4) | copy-done | bytes 262168
  6.6 0.0 copy-start.5
  6.6 0.9 %copy-done.5 = bf16[1,128,1024]{2,1,0:T(8,128)(2,1)S(1)} copy-done((bf16[1,128,1024]{2,1,0:T(8,128)(2,1)S(1)}, bf16[1,128,1024]{2,1,0:T(8,128)(2,1)}, u32[]{:S(2)}) %copy-start.5) | copy-done | bytes 262168
  7.6 0.0 copy-start.6
  7.6 0.8 %copy-done.6 = bf16[512,32]{0,1:T(8,128)(2,1)S(1)} copy-done((bf16[512,32]{0,1:T(8,128)(2,1)S(1)}, bf16[512,32]{0,1:T(8,128)(2,1)}, u32[]{:S(2)}) %copy-start.6) | copy-done | bytes 32792
  8.3 58.3 %shard_map.113 = (bf16[128,1024]{1,0:T(8,128)(2,1)S(1)}, f32[32,512]{1,0:T(8,128)S(1)}) custom-call(bf16[128,4096]{1,0:T(8,128)(2,1)S(1)} %bitcast.11, bf16[32,512]{1,0:T(8,128)(2,1)S(1)} %bitcast.19, bf16[128,2048]{1,0:T(8,128)(2,1)S(1)} %bitcast.12, bf16[128,2048]{1,0:T(8,128)(2,1)S(1)} %bitcast.13, bf16[128,1024]{1,0:T(8,128)(2,1)S(1)} %bitcast.15, ...), custom_call_target="tpu_custom_call" | custom-call | tf_op jit(solution)/shard_map/pallas_call | solution.py:341
  66.7 0.7 %copy.14 = bf16[1,128,1024]{2,1,0:T(8,128)(2,1)} copy(bf16[1,128,1024]{2,1,0:T(8,128)(2,1)S(1)} %bitcast.17) | data formatting | bytes 524288
  67.4 0.6 copy.15
Async XLA Ops:
  0.6 0.7 copy-start.7
  0.6 0.7 copy-start.8
  0.7 0.7 copy-start.9
  1.3 1.2 %copy-start = (bf16[1,128,4096]{2,1,0:T(8,128)(2,1)S(1)}, bf16[1,128,4096]{2,1,0:T(8,128)(2,1)}, u32[]{:S(2)}) copy-start(bf16[1,128,4096]{2,1,0:T(8,128)(2,1)} %param.10) | copy-start | bytes 3145732
  2.5 1.0 %copy-start.1 = (bf16[1,128,2048]{2,1,0:T(8,128)(2,1)S(1)}, bf16[1,128,2048]{2,1,0:T(8,128)(2,1)}, u32[]{:S(2)}) copy-start(bf16[1,128,2048]{2,1,0:T(8,128)(2,1)} %param.12) | copy-start | bytes 1572868
  3.6 1.0 %copy-start.2 = (bf16[1,128,2048]{2,1,0:T(8,128)(2,1)S(1)}, bf16[1,128,2048]{2,1,0:T(8,128)(2,1)}, u32[]{:S(2)}) copy-start(bf16[1,128,2048]{2,1,0:T(8,128)(2,1)} %param.13) | copy-start | bytes 1572868
  4.6 1.0 %copy-start.3 = (bf16[1,1,32,64,128]{4,3,2,1,0:T(8,128)(2,1)S(1)}, bf16[1,1,32,64,128]{4,3,2,1,0:T(8,128)(2,1)}, u32[]{:S(2)}) copy-start(bf16[1,1,32,64,128]{4,3,2,1,0:T(8,128)(2,1)} %param.16) | copy-start | bytes 1572868
  5.7 0.9 %copy-start.4 = (bf16[1,128,1024]{2,1,0:T(8,128)(2,1)S(1)}, bf16[1,128,1024]{2,1,0:T(8,128)(2,1)}, u32[]{:S(2)}) copy-start(bf16[1,128,1024]{2,1,0:T(8,128)(2,1)} %param.14) | copy-start | bytes 786436
  6.6 0.9 %copy-start.5 = (bf16[1,128,1024]{2,1,0:T(8,128)(2,1)S(1)}, bf16[1,128,1024]{2,1,0:T(8,128)(2,1)}, u32[]{:S(2)}) copy-start(bf16[1,128,1024]{2,1,0:T(8,128)(2,1)} %param.15) | copy-start | bytes 786436
  7.6 0.8 %copy-start.6 = (bf16[512,32]{0,1:T(8,128)(2,1)S(1)}, bf16[512,32]{0,1:T(8,128)(2,1)}, u32[]{:S(2)}) copy-start(bf16[512,32]{0,1:T(8,128)(2,1)} %param.11) | copy-start | bytes 98308

commit v3 on v2

--- a/solution.py
+++ b/solution.py
@@ -46,7 +46,7 @@
     is_last = ctx == n_ctx - 1
 
     if fuse:
-        hall, graw_own, graw_all, part, h_send, h_recv, g_send, g_recv, p_all, p_send, p_recv = rest[30:]
+        hall, graw_own, graw_all, part, h_send, h_recv, g_send, g_recv, p_all, p_send, p_recv, mine, final, q_send, q_recv = rest[30:]
 
     fetches = [
         pltpu.make_async_copy(source, target, in_sem.at[i])
@@ -236,7 +236,12 @@
 
     def p_copy(r, peer, slot):
         return pltpu.make_async_remote_copy(
-            src_ref=part, dst_ref=p_all.at[slot], send_sem=p_send.at[r], recv_sem=p_recv.at[r],
+            src_ref=part.at[peer], dst_ref=p_all.at[slot], send_sem=p_send.at[r], recv_sem=p_recv.at[r],
+            device_id=(dp, peer), device_id_type=MESH)
+
+    def q_copy(r, peer, slot):
+        return pltpu.make_async_remote_copy(
+            src_ref=mine, dst_ref=final.at[slot], send_sem=q_send.at[r], recv_sem=q_recv.at[r],
             device_id=(dp, peer), device_id_type=MESH)
 
     if fuse:
@@ -260,18 +265,29 @@
             g_copy(r, lax.rem(dp + r, n_dp), source).wait_recv()
         for d in range(n_dp):
             total = total + mm(jnp.concatenate(split(graw_all[d]), axis=0), hall[d])
-        part[...] = total[:heads] + total[heads:]
+        total = total[:heads] + total[heads:]
+        piece = depth // n_ctx
+        for d in range(n_ctx):
+            part[d] = total[:, d * piece:(d + 1) * piece]
         for r in range(1, n_ctx):
             p_copy(r, lax.rem(ctx + r, n_ctx), ctx).start()
-        p_all[ctx] = part[...]
+        p_all[ctx] = part[ctx]
         for r in range(1, n_ctx):
             p_copy(r, lax.rem(ctx + r, n_ctx), lax.rem(ctx - r + n_ctx, n_ctx)).wait_recv()
         summed = p_all[0]
         for d in range(1, n_ctx):
             summed = summed + p_all[d]
-        out_w[...] = summed
+        mine[...] = summed
+        for r in range(1, n_ctx):
+            q_copy(r, lax.rem(ctx + r, n_ctx), ctx).start()
+        final[ctx] = summed
+        for r in range(1, n_ctx):
+            q_copy(r, lax.rem(ctx + r, n_ctx), lax.rem(ctx - r + n_ctx, n_ctx)).wait_recv()
+        for d in range(n_ctx):
+            out_w[:, d * piece:(d + 1) * piece] = final[d]
         for r in range(1, n_ctx):
             p_copy(r, lax.rem(ctx + r, n_ctx), ctx).wait_send()
+            q_copy(r, lax.rem(ctx + r, n_ctx), ctx).wait_send()
         for r in range(1, n_dp):
             h_copy(r, lax.rem(dp + r, n_dp), dp).wait_send()
             g_copy(r, lax.rem(dp + r, n_dp), dp).wait_send()
@@ -295,7 +311,7 @@
     depth = dt_weight.shape[0]
     heads = step_bias.shape[0]
     gather = depth % 128 == 0
-    fuse = FUSE_END and gather
+    fuse = FUSE_END and depth % (128 * n_ctx) == 0
     hid = hidden[0]
     if gather:
         w = dt_weight.T
@@ -333,9 +349,12 @@
             pltpu.VMEM((n_dp, length, depth), bf16),
             small,
             pltpu.VMEM((n_dp, heads, length), f32),
-            pltpu.VMEM((heads, depth), f32),
+            pltpu.VMEM((n_ctx, heads, depth // n_ctx), f32),
             dma((n_dp,)), dma((n_dp,)), dma((n_dp,)), dma((n_dp,)),
-            pltpu.VMEM((n_ctx, heads, depth), f32),
+            pltpu.VMEM((n_ctx, heads, depth // n_ctx), f32),
+            dma((n_ctx,)), dma((n_ctx,)),
+            pltpu.VMEM((heads, depth // n_ctx), f32),
+            pltpu.VMEM((n_ctx, heads, depth // n_ctx), f32),
             dma((n_ctx,)), dma((n_ctx,)),
         ]
     grad_b, res = pl.pallas_call(
@@ -348,7 +367,7 @@
         out_specs=(vmem, vmem),
         scratch_shapes=scratch,
         compiler_params=pltpu.CompilerParams(
-            collective_id=0, has_side_effects=True, vmem_limit_bytes=48 * 1024 * 1024),
+            collective_id=0, has_side_effects=True, vmem_limit_bytes=63 * 1024 * 1024),
     )(hid, w, ssm_input[0], grad_output[0], b_matrix[0], c_matrix[0],
       stored_states.reshape(heads * HEADDIM, NSTATE), step_bias.reshape(1, heads),
       decay_code.reshape(1, heads), head_group)

time: 68.5 us -> 62.9 us (0.918)
  local copies, waits for them, and re-layouts: 9 us -> 2.33 us
  Pallas kernels: 58.3 us -> 59.7 us
    unnamed x22 -> x4, local copies, waits for them, and re-layouts: 9 us -> 2.33 us
    pallas_call x1, Pallas kernels: 58.3 us -> 59.7 us  [body(): pl.pallas_call(functools.partial(kernel, (n_dp, n_ctx, gather, fuse)), ou...]
where the time goes in v3:
time: 62.9 us; the launch traced here: 62.7 us
  Pallas kernels  59.7 us (95%)
  local copies, waits for them, and re-layouts  2.33 us (4%)
  between operations  0.65 us (1%)
    pallas_call x1, Pallas kernels, body(): pl.pallas_call(functools.partial(kernel, (n_dp, n_ctx, gather, fuse)), ou...  59.7 us
    unnamed x4, local copies, waits for them, and re-layouts  2.33 us

profile of v3, /device:TPU:0, one launch (start us, length us, event | category | flops | bytes accessed | tf_op | source)
XLA Modules:
  0.0 62.7 jit_solution(4513543532776612892)
XLA Ops:
  0.6 59.7 %shard_map.113 = (bf16[128,1024]{1,0:T(8,128)(2,1)}, f32[32,512]{1,0:T(8,128)}) custom-call(bf16[128,4096]{1,0:T(8,128)(2,1)} %bitcast.11, bf16[32,512]{1,0:T(8,128)(2,1)} %bitcast.19, bf16[128,2048]{1,0:T(8,128)(2,1)} %bitcast.12, bf16[128,2048]{1,0:T(8,128)(2,1)} %bitcast.13, bf16[128,1024]{1,0:T(8,128)(2,1)} %bitcast.15, bf16[128,1024]{1,0:T(8,128)(2,1)} %bitcast.16, ...), custom_call_target="tpu_custom_call" | custom-call | tf_op jit(solution)/shard_map/pallas_call | solution.py:360
  60.4 0.0 copy-start
  60.4 1.7 %copy.14 = bf16[1,128,1024]{2,1,0:T(8,128)(2,1)} copy(bf16[1,128,1024]{2,1,0:T(8,128)(2,1)} %bitcast.17) | data formatting | bytes 524288
  62.1 0.0 copy-done
  62.1 0.6 %copy.15 = f32[512,32]{0,1:T(8,128)} copy(f32[512,32]{0,1:T(8,128)S(1)} %bitcast.18) | data formatting | bytes 131072
Async XLA Ops:
  60.4 1.7 %copy-start = (f32[32,512]{1,0:T(8,128)S(1)}, f32[32,512]{1,0:T(8,128)}, u32[]{:S(2)}) copy-start(f32[32,512]{1,0:T(8,128)} %get-tuple-element.5) | copy-start | bytes 196612

commit v4 on v3

--- a/solution.py
+++ b/solution.py
@@ -132,7 +132,7 @@
     elast_s[...] = jnp.exp(last)
 
     def chain(k):
-        span = pl.ds(pl.multiple_of(k * (CHUNK_HEADS * HEADDIM), CHUNK_HEADS * HEADDIM), CHUNK_HEADS * HEADDIM)
+        span = pl.ds(pl.multiple_of(k * HEADDIM, HEADDIM), HEADDIM)
         return pltpu.make_async_remote_copy(
             src_ref=send_s.at[span], dst_ref=recv_s.at[span], send_sem=ch_send.at[k], recv_sem=ch_recv.at[k],
             device_id=(dp, lax.rem(ctx - 1 + n_ctx, n_ctx)), device_id_type=MESH)
@@ -145,9 +145,9 @@
             both = mm(jnp.concatenate(split(weighted), axis=0), cg2[hg[h], :length, :])
             send_s[span, :] = both[:HEADDIM] + both[HEADDIM:]
 
-        @pl.when(is_last)
-        def _():
-            chain(k).start()
+            @pl.when(is_last)
+            def _():
+                chain(h).start()
 
         return carry
 
@@ -163,17 +163,18 @@
     ones = jnp.ones((8, 256), bf16)
 
     def main_chunk(k, carry):
-        @pl.when(ctx < n_ctx - 1)
-        def _():
-            chain(k).wait_recv()
-
-        @pl.when(jnp.logical_and(ctx < n_ctx - 1, ctx > 0))
-        def _():
-            for e in range(CHUNK_HEADS):
-                h = k * CHUNK_HEADS + e
-                span = pl.ds(pl.multiple_of(h * HEADDIM, HEADDIM), HEADDIM)
+        for e in range(CHUNK_HEADS):
+            h = k * CHUNK_HEADS + e
+            span = pl.ds(pl.multiple_of(h * HEADDIM, HEADDIM), HEADDIM)
+
+            @pl.when(ctx < n_ctx - 1)
+            def _():
+                chain(h).wait_recv()
+
+            @pl.when(jnp.logical_and(ctx < n_ctx - 1, ctx > 0))
+            def _():
                 send_s[span, :] = send_s[span, :] + elast_s[pl.ds(h, 1), :] * recv_s[span, :]
-            chain(k).start()
+                chain(h).start()
 
         grads = []
         for q in range(CHUNK_HEADS // 2):
@@ -302,7 +303,7 @@
             chain(k).wait_send()
             return carry
 
-        lax.fori_loop(0, chunks, drain, 0)
+        lax.fori_loop(0, heads, drain, 0)
 
 
 def body(n_dp, n_ctx, hidden, dt_weight, ssm_input, grad_output, b_matrix, c_matrix,
@@ -317,7 +318,6 @@
         w = dt_weight.T
     else:
         w = lax.all_gather(dt_weight.T, "dp", axis=0, tiled=False)
-    chunks = heads // CHUNK_HEADS
     any_ = pl.BlockSpec(memory_space=pltpu.HBM)
     vmem = pl.BlockSpec(memory_space=pltpu.VMEM)
     small = pltpu.VMEM((heads, length), f32)
@@ -342,7 +342,7 @@
         pltpu.VMEM(c_matrix.shape[1:], bf16),
         pltpu.VMEM((heads * HEADDIM, NSTATE), bf16),
         dma((7,)),
-        dma((n_dp,)), dma((n_dp,)), dma((chunks,)), dma((chunks,)),
+        dma((n_dp,)), dma((n_dp,)), dma((heads,)), dma((heads,)),
     ]
     if fuse:
         scratch += [

time: 62.9 us -> 64.3 us (1.022)
  Pallas kernels: 59.7 us -> 61.2 us
    pallas_call x1, Pallas kernels: 59.7 us -> 61.2 us  [body(): pl.pallas_call(functools.partial(kernel, (n_dp, n_ctx, gather, fuse)), ou...]
where the time goes in v4:
time: 64.3 us; the launch traced here: 64.1 us
  Pallas kernels  61.2 us (95%)
  local copies, waits for them, and re-layouts  2.33 us (4%)
  between operations  0.65 us (1%)
    pallas_call x1, Pallas kernels, body(): pl.pallas_call(functools.partial(kernel, (n_dp, n_ctx, gather, fuse)), ou...  61.2 us
    unnamed x4, local copies, waits for them, and re-layouts  2.33 us

profile of v4, /device:TPU:0, one launch (start us, length us, event | category | flops | bytes accessed | tf_op | source)
XLA Modules:
  0.0 64.1 jit_solution(10622980710409949096)
XLA Ops:
  0.6 61.2 %shard_map.113 = (bf16[128,1024]{1,0:T(8,128)(2,1)}, f32[32,512]{1,0:T(8,128)}) custom-call(bf16[128,4096]{1,0:T(8,128)(2,1)} %bitcast.11, bf16[32,512]{1,0:T(8,128)(2,1)} %bitcast.19, bf16[128,2048]{1,0:T(8,128)(2,1)} %bitcast.12, bf16[128,2048]{1,0:T(8,128)(2,1)} %bitcast.13, bf16[128,1024]{1,0:T(8,128)(2,1)} %bitcast.15, bf16[128,1024]{1,0:T(8,128)(2,1)} %bitcast.16, ...), custom_call_target="tpu_custom_call" | custom-call | tf_op jit(solution)/shard_map/pallas_call | solution.py:360
  61.8 0.0 copy-start
  61.8 1.7 %copy.14 = bf16[1,128,1024]{2,1,0:T(8,128)(2,1)} copy(bf16[1,128,1024]{2,1,0:T(8,128)(2,1)} %bitcast.17) | data formatting | bytes 524288
  63.5 0.0 copy-done
  63.5 0.6 copy.15
Async XLA Ops:
  61.8 1.7 %copy-start = (f32[32,512]{1,0:T(8,128)S(1)}, f32[32,512]{1,0:T(8,128)}, u32[]{:S(2)}) copy-start(f32[32,512]{1,0:T(8,128)} %get-tuple-element.5) | copy-start | bytes 196612

commit v5 on v3

--- a/solution.py
+++ b/solution.py
@@ -83,9 +83,6 @@
     if gather:
         for r in range(1, n_dp):
             w_copy(r, lax.rem(dp + r, n_dp), dp).start()
-    if fuse:
-        for r in range(1, n_dp):
-            h_copy(r, lax.rem(dp + r, n_dp), dp).start()
 
     fetches[0].wait()
     for k in range(x.shape[1] // 128):
@@ -115,6 +112,9 @@
         own_w.wait()
         for r in range(1, n_dp):
             w_copy(r, lax.rem(dp + r, n_dp), lax.rem(dp - r + n_dp, n_dp)).wait_recv()
+    if fuse:
+        for r in range(1, n_dp):
+            h_copy(r, lax.rem(dp + r, n_dp), dp).start()
     proj = jnp.zeros((heads, length), f32)
     for d in range(n_dp):
         proj = proj + mm_nt(wall[d] if gather else w[d], hid[:, d * depth:(d + 1) * depth])

time: 62.9 us -> 62.4 us (level)
  no operation moved by 1% of the time
where the time goes in v5:
time: 62.4 us; the launch traced here: 62.2 us
  Pallas kernels  59.2 us (95%)
  local copies, waits for them, and re-layouts  2.33 us (4%)
  between operations  0.65 us (1%)
    pallas_call x1, Pallas kernels, body(): pl.pallas_call(functools.partial(kernel, (n_dp, n_ctx, gather, fuse)), ou...  59.2 us
    unnamed x4, local copies, waits for them, and re-layouts  2.33 us

profile of v5, /device:TPU:0, one launch (start us, length us, event | category | flops | bytes accessed | tf_op | source)
XLA Modules:
  0.0 62.2 jit_solution(14080457476353483074)
XLA Ops:
  0.6 59.2 %shard_map.113 = (bf16[128,1024]{1,0:T(8,128)(2,1)}, f32[32,512]{1,0:T(8,128)}) custom-call(bf16[128,4096]{1,0:T(8,128)(2,1)} %bitcast.11, bf16[32,512]{1,0:T(8,128)(2,1)} %bitcast.19, bf16[128,2048]{1,0:T(8,128)(2,1)} %bitcast.12, bf16[128,2048]{1,0:T(8,128)(2,1)} %bitcast.13, bf16[128,1024]{1,0:T(8,128)(2,1)} %bitcast.15, bf16[128,1024]{1,0:T(8,128)(2,1)} %bitcast.16, ...), custom_call_target="tpu_custom_call" | custom-call | tf_op jit(solution)/shard_map/pallas_call | solution.py:360
  59.9 0.0 copy-start
  59.9 1.7 %copy.14 = bf16[1,128,1024]{2,1,0:T(8,128)(2,1)} copy(bf16[1,128,1024]{2,1,0:T(8,128)(2,1)} %bitcast.17) | data formatting | bytes 524288
  61.6 0.0 copy-done
  61.6 0.6 %copy.15 = f32[512,32]{0,1:T(8,128)} copy(f32[512,32]{0,1:T(8,128)S(1)} %bitcast.18) | data formatting | bytes 131072
Async XLA Ops:
  59.9 1.7 %copy-start = (f32[32,512]{1,0:T(8,128)S(1)}, f32[32,512]{1,0:T(8,128)}, u32[]{:S(2)}) copy-start(f32[32,512]{1,0:T(8,128)} %get-tuple-element.5) | copy-start | bytes 196612
